TPU v7x, 32 devices: a whole 2x2x4 slice. The times are simulated.
32 devices in a mesh: group: 4 (over z), head: 2 (over core), batch: 4 (over y, x).
Axes of the slice: x: 2, y: 2, z: 4, core: 2. Of those that a mesh axis runs over, the one named last changes fastest.
Arguments:
- queries: bfloat16 [2048, 1536], P(('batch', 'group'), 'head'), parts along dimension 0, may hold values from -6 to 6
- keys: bfloat16 [2048, 1536], P(('batch', 'group'), 'head'), parts along dimension 0, may hold values from -6 to 6
- values: bfloat16 [2048, 1536], P(('batch', 'group'), 'head'), parts along dimension 0, may hold values from -6 to 6
- grad_out: bfloat16 [2048, 1536], P(('batch', 'group'), 'head'), parts along dimension 0, may hold values from -6 to 6
- lengths: int32 [32], P('batch'), parts along dimension 0, may hold values from 20 to 64, as said below
Outputs:
- grad_queries: bfloat16 [2048, 1536], P(('batch', 'group'), 'head'), parts along dimension 0
- grad_keys: bfloat16 [2048, 1536], P(('batch', 'group'), 'head'), parts along dimension 0
- grad_values: bfloat16 [2048, 1536], P(('batch', 'group'), 'head'), parts along dimension 0
There are 4 independent parts, one for each index of `batch`. A program takes and returns all parts, laid end to end along the dimension named above; each array names one. Nothing has to cross between parts.
Inputs may be any that keep to these rules, and one draw needn't show every extreme that they name: `lengths`: in every draw some span is full, with 64 valid tokens.
All inputs are finite; a program needn't handle non-finite values.
Results may differ from a plain program's by a relative error of at most 0.022.
Values may be sent and summed in bfloat16 or wider, within the bound.
A program may use at most 64 MiB of HBM per device.

v0:
```python
import math

import jax
import jax.numpy as jnp
from jax import lax
from jax.sharding import PartitionSpec as P

HD = 128


masked_score = -1e30


def passed_along(block, axis, distance):
    devices = range(lax.axis_size(axis))
    route = [((i - distance) % len(devices), i) for i in devices]
    return lax.ppermute(block, axis, route)


def lookup_length(span_ids, lengths):
    table = jnp.arange(lengths.shape[0], dtype=jnp.int32)
    return jnp.sum(jnp.where(span_ids[:, None] == table[None, :], lengths[None, :], 0), axis=1)


def heads_first(matrix, head_count):
    return matrix.reshape(matrix.shape[0], head_count, HD).transpose(1, 0, 2)


def rows_first(tensor):
    return tensor.transpose(1, 0, 2).reshape(tensor.shape[1], tensor.shape[0] * tensor.shape[2])


def body(queries, keys, values, grad_out, lengths):
    row_count, feature_count = queries.shape
    head_count = feature_count // HD
    slice_count = lax.axis_size("group")
    my_slice = lax.axis_index("group")
    score_scale = 1.0 / math.sqrt(HD)
    gathered_keys, gathered_values = (
        lax.all_gather(keys, "group", axis=0, tiled=True),
        lax.all_gather(values, "group", axis=0, tiled=True),
    )
    key_count = gathered_keys.shape[0]
    span_len = key_count // lengths.shape[0]
    key_index = jnp.arange(key_count, dtype=jnp.int32)
    key_span = key_index // span_len
    key_valid = key_index % span_len < lookup_length(key_span, lengths)
    own_index = my_slice * row_count + jnp.arange(row_count, dtype=jnp.int32)
    own_span = own_index // span_len
    own_valid = own_index % span_len < lookup_length(own_span, lengths)
    grad_kept = jnp.where(own_valid[:, None], grad_out, jnp.zeros_like(grad_out))
    top_span = jnp.max(own_span)
    query_heads = heads_first(queries, head_count)
    grad_heads = heads_first(grad_kept, head_count)
    key_heads = heads_first(gathered_keys, head_count)
    value_heads = heads_first(gathered_values, head_count)
    visible = (key_span[None, :] <= own_span[:, None]) & key_valid[None, :]

    def row_stats(head_parts):
        query_head, grad_head, key_head, value_head = head_parts
        scores = (
            jnp.einsum("rd,kd->rk", query_head, key_head, preferred_element_type=jnp.float32)
            * score_scale
        )
        scores = jnp.where(visible, scores, masked_score)
        row_max = jnp.max(scores, axis=1, keepdims=True)
        unnormed = jnp.exp(scores - row_max)
        row_sum = jnp.sum(unnormed, axis=1, keepdims=True)
        probs_low = (unnormed / row_sum).astype(jnp.bfloat16)
        attended = jnp.dot(probs_low, value_head, preferred_element_type=jnp.float32).astype(
            jnp.bfloat16
        )
        row_delta = jnp.sum(grad_head.astype(jnp.float32) * attended.astype(jnp.float32), axis=1)
        return (row_max[:, 0], row_sum[:, 0], row_delta)

    row_max, row_sum, row_delta = lax.map(
        row_stats, (query_heads, grad_heads, key_heads, value_heads)
    )

    def dense_terms(block):
        start = block * row_count
        key_block = lax.dynamic_slice_in_dim(key_heads, start, row_count, 1)
        value_block = lax.dynamic_slice_in_dim(value_heads, start, row_count, 1)
        valid_block = lax.dynamic_slice_in_dim(key_valid, start, row_count, 0)
        span_block = lax.dynamic_slice_in_dim(key_span, start, row_count, 0)
        block_mask = (span_block[None, :] <= own_span[:, None]) & valid_block[None, :]
        scores = (
            jnp.einsum("hrd,hkd->hrk", query_heads, key_block, preferred_element_type=jnp.float32)
            * score_scale
        )
        scores = jnp.where(block_mask[None], scores, masked_score)
        probs = jnp.exp(scores - row_max[:, :, None]) / row_sum[:, :, None]
        probs_low = probs.astype(jnp.bfloat16)
        prob_grad = jnp.einsum(
            "hrd,hkd->hrk", grad_heads, value_block, preferred_element_type=jnp.float32
        )
        score_grad = (probs * (prob_grad - row_delta[:, :, None])).astype(jnp.bfloat16)
        query_term = jnp.einsum(
            "hrk,hkd->hrd", score_grad, key_block, preferred_element_type=jnp.float32
        )
        key_term = rows_first(
            jnp.einsum("hrk,hrd->hkd", score_grad, query_heads, preferred_element_type=jnp.float32)
            * score_scale
        )
        value_term = rows_first(
            jnp.einsum("hrk,hrd->hkd", probs_low, grad_heads, preferred_element_type=jnp.float32)
        )
        return (query_term, key_term, value_term)

    def empty_terms(block):
        query_term = jnp.zeros((head_count, row_count, HD), jnp.float32)
        other_term = jnp.zeros((row_count, feature_count), jnp.float32)
        return (query_term, other_term, other_term)

    def block_terms(block):
        first_span = block * row_count // span_len
        return lax.cond(first_span <= top_span, dense_terms, empty_terms, block)

    query_zero = jnp.zeros((head_count, row_count, HD), jnp.float32)

    def chain_step(block_step, loop_state):
        query_grad, travel = loop_state
        block = (my_slice - block_step) % slice_count
        query_term, key_term, value_term = block_terms(block)
        travel = travel + jnp.stack([key_term, value_term])
        travel = passed_along(travel.astype(jnp.bfloat16), "group", 1).astype(travel.dtype)
        return (query_grad + query_term, travel)

    travel_zero = jnp.zeros((2, row_count, feature_count), jnp.float32)
    query_grad, travel = lax.fori_loop(0, slice_count, chain_step, (query_zero, travel_zero))
    key_grad = travel[0]
    value_grad = travel[1]
    query_low = rows_first(query_grad * score_scale).astype(jnp.bfloat16)
    return (query_low, key_grad.astype(jnp.bfloat16), value_grad.astype(jnp.bfloat16))


def solution(mesh):
    return jax.shard_map(
        body,
        mesh=mesh,
        in_specs=(
            P(("batch", "group"), "head"),
            P(("batch", "group"), "head"),
            P(("batch", "group"), "head"),
            P(("batch", "group"), "head"),
            P("batch"),
        ),
        out_specs=(
            P(("batch", "group"), "head"),
            P(("batch", "group"), "head"),
            P(("batch", "group"), "head"),
        ),
        check_vma=False,
    )
```

profile of v0, /device:TPU:0, one launch (start us, length us, event | category | flops | bytes accessed | tf_op | source)
XLA Modules:
  0.0 119.7 jit_solution(12962529779978384315)
XLA Ops:
  0.6 0.7 and_select_fusion.1
  1.4 0.7 copy-done.3
  2.1 1.0 broadcast_select_fusion
  3.4 0.6 copy-done
  4.2 20.5 %all_gather.7 = bf16[512,768]{0,1:T(8,128)(2,1)S(1)} all-gather(bf16[128,768]{0,1:T(8,128)(2,1)S(1)} %copy.50), channel_id=1, replica_groups=mesh['group'=4,'head'=2,'batch'=4] {'group'}, dimensions={0}, use_global_device_ids=true | all-gather | bytes 983040 | tf_op jit(solution)/shard_map/all_gather | solution.py:41
  24.7 1.2 copy.53
  26.1 17.0 %all_gather.6 = bf16[512,768]{0,1:T(8,128)(2,1)S(1)} all-gather(bf16[128,768]{0,1:T(8,128)(2,1)S(1)} %copy.47), channel_id=1, replica_groups=mesh['group'=4,'head'=2,'batch'=4] {'group'}, dimensions={0}, use_global_device_ids=true | all-gather | bytes 983040 | tf_op jit(solution)/shard_map/all_gather | solution.py:40
  43.1 1.2 copy.54
  44.5 16.4 %while.33 = (s32[]{:T(128)}, f32[6,128]{1,0:T(8,128)S(1)}, f32[6,128]{1,0:T(8,128)S(1)}, f32[6,128]{1,0:T(8,128)S(1)}, bf16[6,128,128]{1,2,0:T(8,128)(2,1)S(1)},...) while((s32[]{:T(128)}, f32[6,128]{1,0:T(8,128)S(1)}, ...), condition=%wide.region_7.8_spmd.clone, body=%wide.region_3.7_spmd.clone.sunk | while | flops 34291328 | bytes 1125513 | solution.py:76
  44.5 1.2 %fusion.61 = (f32[128]{0:T(128)S(1)}, f32[128,512]{1,0:T(8,128)S(1)}) fusion(bf16[6,512,128]{2,1,0:T(8,128)(2,1)} %get-tuple-element.902, s32[]{:T(128)} %get-tuple-element.884, bf16[6,128,128]{1,2,0:T(8,128)(2,1)S(1)} %get-tuple-element.901, pred[512]{0:T(512)(128)(4,1)S(1)} %get-tuple-element.907, s32[128]{0:T(128)S(1)} %get-tuple-element.905, ...), kind=kOutput, calls=%fused_computation.85.clone.1 | convolution fusion | flops 17104768 | bytes 430592 | tf_op jit(solution)/shard_map/while/body/eval_jaxpr/rd,kd->rk/dot_general | solution.py:62
  45.7 0.2 fusion.62
  45.9 1.2 %fusion.63 = f32[128]{0:T(128)S(1)} fusion(bf16[6,512,128]{2,1,0:T(8,128)(2,1)} %get-tuple-element.904, s32[]{:T(128)} %get-tuple-element.884, f32[128,512]{1,0:T(8,128)S(1)} %get-tuple-element.845, f32[128]{0:T(128)S(1)} %fusion.62, f32[128]{0:T(128)S(1)} %get-tuple-element.844, bf16[6,128,128]{1,2,0:T(8,128)(2,1)S(1)} %get-tuple-element.903), kind=kOutput, calls=%fused_computation.37.clone.1 | convolution fusion | flops 17055616 | bytes 428544 | tf_op jit(solution)/shard_map/while/body/eval_jaxpr/dot_general | solution.py:70
  47.2 1.2 %fusion.61 = (f32[128]{0:T(128)S(1)}, f32[128,512]{1,0:T(8,128)S(1)}) fusion(bf16[6,512,128]{2,1,0:T(8,128)(2,1)} %get-tuple-element.902, s32[]{:T(128)} %get-tuple-element.884, bf16[6,128,128]{1,2,0:T(8,128)(2,1)S(1)} %get-tuple-element.901, pred[512]{0:T(512)(128)(4,1)S(1)} %get-tuple-element.907, s32[128]{0:T(128)S(1)} %get-tuple-element.905, ...), kind=kOutput, calls=%fused_computation.85.clone.1 | convolution fusion | flops 17104768 | bytes 430592 | tf_op jit(solution)/shard_map/while/body/eval_jaxpr/rd,kd->rk/dot_general | solution.py:62
  48.6 1.2 %fusion.63 = f32[128]{0:T(128)S(1)} fusion(bf16[6,512,128]{2,1,0:T(8,128)(2,1)} %get-tuple-element.904, s32[]{:T(128)} %get-tuple-element.884, f32[128,512]{1,0:T(8,128)S(1)} %get-tuple-element.845, f32[128]{0:T(128)S(1)} %fusion.62, f32[128]{0:T(128)S(1)} %get-tuple-element.844, bf16[6,128,128]{1,2,0:T(8,128)(2,1)S(1)} %get-tuple-element.903), kind=kOutput, calls=%fused_computation.37.clone.1 | convolution fusion | flops 17055616 | bytes 428544 | tf_op jit(solution)/shard_map/while/body/eval_jaxpr/dot_general | solution.py:70
  49.9 1.2 %fusion.61 = (f32[128]{0:T(128)S(1)}, f32[128,512]{1,0:T(8,128)S(1)}) fusion(bf16[6,512,128]{2,1,0:T(8,128)(2,1)} %get-tuple-element.902, s32[]{:T(128)} %get-tuple-element.884, bf16[6,128,128]{1,2,0:T(8,128)(2,1)S(1)} %get-tuple-element.901, pred[512]{0:T(512)(128)(4,1)S(1)} %get-tuple-element.907, s32[128]{0:T(128)S(1)} %get-tuple-element.905, ...), kind=kOutput, calls=%fused_computation.85.clone.1 | convolution fusion | flops 17104768 | bytes 430592 | tf_op jit(solution)/shard_map/while/body/eval_jaxpr/rd,kd->rk/dot_general | solution.py:62
  51.3 1.2 %fusion.63 = f32[128]{0:T(128)S(1)} fusion(bf16[6,512,128]{2,1,0:T(8,128)(2,1)} %get-tuple-element.904, s32[]{:T(128)} %get-tuple-element.884, f32[128,512]{1,0:T(8,128)S(1)} %get-tuple-element.845, f32[128]{0:T(128)S(1)} %fusion.62, f32[128]{0:T(128)S(1)} %get-tuple-element.844, bf16[6,128,128]{1,2,0:T(8,128)(2,1)S(1)} %get-tuple-element.903), kind=kOutput, calls=%fused_computation.37.clone.1 | convolution fusion | flops 17055616 | bytes 428544 | tf_op jit(solution)/shard_map/while/body/eval_jaxpr/dot_general | solution.py:70
  52.6 1.2 %fusion.61 = (f32[128]{0:T(128)S(1)}, f32[128,512]{1,0:T(8,128)S(1)}) fusion(bf16[6,512,128]{2,1,0:T(8,128)(2,1)} %get-tuple-element.902, s32[]{:T(128)} %get-tuple-element.884, bf16[6,128,128]{1,2,0:T(8,128)(2,1)S(1)} %get-tuple-element.901, pred[512]{0:T(512)(128)(4,1)S(1)} %get-tuple-element.907, s32[128]{0:T(128)S(1)} %get-tuple-element.905, ...), kind=kOutput, calls=%fused_computation.85.clone.1 | convolution fusion | flops 17104768 | bytes 430592 | tf_op jit(solution)/shard_map/while/body/eval_jaxpr/rd,kd->rk/dot_general | solution.py:62
  53.9 0.2 fusion.62
  54.1 1.2 %fusion.63 = f32[128]{0:T(128)S(1)} fusion(bf16[6,512,128]{2,1,0:T(8,128)(2,1)} %get-tuple-element.904, s32[]{:T(128)} %get-tuple-element.884, f32[128,512]{1,0:T(8,128)S(1)} %get-tuple-element.845, f32[128]{0:T(128)S(1)} %fusion.62, f32[128]{0:T(128)S(1)} %get-tuple-element.844, bf16[6,128,128]{1,2,0:T(8,128)(2,1)S(1)} %get-tuple-element.903), kind=kOutput, calls=%fused_computation.37.clone.1 | convolution fusion | flops 17055616 | bytes 428544 | tf_op jit(solution)/shard_map/while/body/eval_jaxpr/dot_general | solution.py:70
  55.4 1.2 %fusion.61 = (f32[128]{0:T(128)S(1)}, f32[128,512]{1,0:T(8,128)S(1)}) fusion(bf16[6,512,128]{2,1,0:T(8,128)(2,1)} %get-tuple-element.902, s32[]{:T(128)} %get-tuple-element.884, bf16[6,128,128]{1,2,0:T(8,128)(2,1)S(1)} %get-tuple-element.901, pred[512]{0:T(512)(128)(4,1)S(1)} %get-tuple-element.907, s32[128]{0:T(128)S(1)} %get-tuple-element.905, ...), kind=kOutput, calls=%fused_computation.85.clone.1 | convolution fusion | flops 17104768 | bytes 430592 | tf_op jit(solution)/shard_map/while/body/eval_jaxpr/rd,kd->rk/dot_general | solution.py:62
  56.6 0.2 fusion.62
  56.8 1.2 %fusion.63 = f32[128]{0:T(128)S(1)} fusion(bf16[6,512,128]{2,1,0:T(8,128)(2,1)} %get-tuple-element.904, s32[]{:T(128)} %get-tuple-element.884, f32[128,512]{1,0:T(8,128)S(1)} %get-tuple-element.845, f32[128]{0:T(128)S(1)} %fusion.62, f32[128]{0:T(128)S(1)} %get-tuple-element.844, bf16[6,128,128]{1,2,0:T(8,128)(2,1)S(1)} %get-tuple-element.903), kind=kOutput, calls=%fused_computation.37.clone.1 | convolution fusion | flops 17055616 | bytes 428544 | tf_op jit(solution)/shard_map/while/body/eval_jaxpr/dot_general | solution.py:70
  58.1 1.2 %fusion.61 = (f32[128]{0:T(128)S(1)}, f32[128,512]{1,0:T(8,128)S(1)}) fusion(bf16[6,512,128]{2,1,0:T(8,128)(2,1)} %get-tuple-element.902, s32[]{:T(128)} %get-tuple-element.884, bf16[6,128,128]{1,2,0:T(8,128)(2,1)S(1)} %get-tuple-element.901, pred[512]{0:T(512)(128)(4,1)S(1)} %get-tuple-element.907, s32[128]{0:T(128)S(1)} %get-tuple-element.905, ...), kind=kOutput, calls=%fused_computation.85.clone.1 | convolution fusion | flops 17104768 | bytes 430592 | tf_op jit(solution)/shard_map/while/body/eval_jaxpr/rd,kd->rk/dot_general | solution.py:62
  59.3 0.2 fusion.62
  59.5 1.2 %fusion.63 = f32[128]{0:T(128)S(1)} fusion(bf16[6,512,128]{2,1,0:T(8,128)(2,1)} %get-tuple-element.904, s32[]{:T(128)} %get-tuple-element.884, f32[128,512]{1,0:T(8,128)S(1)} %get-tuple-element.845, f32[128]{0:T(128)S(1)} %fusion.62, f32[128]{0:T(128)S(1)} %get-tuple-element.844, bf16[6,128,128]{1,2,0:T(8,128)(2,1)S(1)} %get-tuple-element.903), kind=kOutput, calls=%fused_computation.37.clone.1 | convolution fusion | flops 17055616 | bytes 428544 | tf_op jit(solution)/shard_map/while/body/eval_jaxpr/dot_general | solution.py:70
  60.8 0.5 copy-done.4
  61.4 0.6 copy-done.5
  62.0 55.7 %while.34 = (s32[]{:T(128)}, f32[6,128,128]{2,1,0:T(8,128)S(1)}, f32[2,128,768]{1,2,0:T(8,128)S(1)}, s32[]{:T(128)}, s32[]{:T(128)}, /*index=5*/pred[512]{0:T(51...) while((s32[]{:T(128)}, f32[6,128,128]{2,1,0:T(8,128)S(1)}, ...), condition=%wide.region_11.12_spmd.clone, body=%wide.region_8.11_spmd.clone.sunk | while | flops 127933216 | bytes 11126919 | solution.py:130
  62.8 4.5 %conditional.3 = (f32[6,128,128]{2,1,0:T(8,128)S(1)}, f32[1,128,768]{1,2,0:T(8,128)S(1)}, f32[1,128,768]{1,2,0:T(8,128)S(1)}) conditional(s32[]{:T(128)} %convert_element_type.110, () %tuple.92, (s32[]{:T(128)}, s32[512]{0:T(512)S(1)}, s32[128]{0:T(128)S(1)}, pred[512]{0:T(512)(128)(4,1)S(1)}, bf16[6,512,128]{2,1,0:T(8,128)(2,1)}, ...), branch_computations={%region_9.9_spmd, %region_10.10_spmd} | conditional | flops 126751232 | bytes 5170290 | solution.py:117
  63.1 1.2 fusion.12
  64.3 1.1 fusion.14
  65.4 1.2 %fusion.18 = f32[6,128,128]{2,1,0:T(8,128)S(1)} fusion(bf16[6,128,128]{1,2,0:T(8,128)(2,1)S(1)} %fusion.14, bf16[6,512,128]{2,1,0:T(8,128)(2,1)} %get-tuple-element.416, s32[]{:T(128)S(6)} %select_n.90), kind=kOutput, calls=%fused_computation.18 | convolution fusion | flops 25165824 | bytes 786436 | tf_op jit(solution)/shard_map/while/body/eval_jaxpr/cond/branch_1_fun/hrk,hkd->hrd/dot_general | solution.py:98
  66.6 0.3 fusion.6
  67.1 0.3 fusion.15
  67.4 0.9 collective-permute-start
  68.5 8.6 %collective-permute-done = bf16[2,128,768]{1,2,0:T(8,128)(2,1)S(1)} collective-permute-done((bf16[2,128,768]{1,2,0:T(8,128)(2,1)S(1)}, bf16[2,128,768]{1,2,0:T(8,128)(2,1)S(1)}, u32[]{:S(2)}, u32[]{:S(2)}) %collective-permute-start) | collective-permute-done | bytes 393248 | tf_op jit(solution)/shard_map/while/body/eval_jaxpr/ppermute | solution.py:17
  77.1 0.7 copy-done.10
  78.9 3.5 %collective-permute-start = (bf16[2,128,768]{1,2,0:T(8,128)(2,1)S(1)}, bf16[2,128,768]{1,2,0:T(8,128)(2,1)S(1)}, u32[]{:S(2)}, u32[]{:S(2)}) collective-permute-start(bf16[2,128,768]{1,2,0:T(8,128)(2,1)S(1)} %fusion.64), channel_id=1, source_target_pairs={{24,0},{0,8},{8,16},{16,24},{25,1},{1,9},{9,17},{17,25},{26,2},{2,... | collective-permute-start | bytes 1179656 | tf_op jit(solution)/shard_map/while/body/eval_jaxpr/ppermute | solution.py:17
  82.5 7.3 %collective-permute-done = bf16[2,128,768]{1,2,0:T(8,128)(2,1)S(1)} collective-permute-done((bf16[2,128,768]{1,2,0:T(8,128)(2,1)S(1)}, bf16[2,128,768]{1,2,0:T(8,128)(2,1)S(1)}, u32[]{:S(2)}, u32[]{:S(2)}) %collective-permute-start) | collective-permute-done | bytes 393248 | tf_op jit(solution)/shard_map/while/body/eval_jaxpr/ppermute | solution.py:17
  90.0 0.7 copy-done.10
  91.7 2.5 %collective-permute-start = (bf16[2,128,768]{1,2,0:T(8,128)(2,1)S(1)}, bf16[2,128,768]{1,2,0:T(8,128)(2,1)S(1)}, u32[]{:S(2)}, u32[]{:S(2)}) collective-permute-start(bf16[2,128,768]{1,2,0:T(8,128)(2,1)S(1)} %fusion.64), channel_id=1, source_target_pairs={{24,0},{0,8},{8,16},{16,24},{25,1},{1,9},{9,17},{17,25},{26,2},{2,... | collective-permute-start | bytes 1179656 | tf_op jit(solution)/shard_map/while/body/eval_jaxpr/ppermute | solution.py:17
  94.4 8.5 %collective-permute-done = bf16[2,128,768]{1,2,0:T(8,128)(2,1)S(1)} collective-permute-done((bf16[2,128,768]{1,2,0:T(8,128)(2,1)S(1)}, bf16[2,128,768]{1,2,0:T(8,128)(2,1)S(1)}, u32[]{:S(2)}, u32[]{:S(2)}) %collective-permute-start) | collective-permute-done | bytes 393248 | tf_op jit(solution)/shard_map/while/body/eval_jaxpr/ppermute | solution.py:17
  102.9 0.7 copy-done.10
  104.7 2.5 %collective-permute-start = (bf16[2,128,768]{1,2,0:T(8,128)(2,1)S(1)}, bf16[2,128,768]{1,2,0:T(8,128)(2,1)S(1)}, u32[]{:S(2)}, u32[]{:S(2)}) collective-permute-start(bf16[2,128,768]{1,2,0:T(8,128)(2,1)S(1)} %fusion.64), channel_id=1, source_target_pairs={{24,0},{0,8},{8,16},{16,24},{25,1},{1,9},{9,17},{17,25},{26,2},{2,... | collective-permute-start | bytes 1179656 | tf_op jit(solution)/shard_map/while/body/eval_jaxpr/ppermute | solution.py:17
  107.2 9.7 %collective-permute-done = bf16[2,128,768]{1,2,0:T(8,128)(2,1)S(1)} collective-permute-done((bf16[2,128,768]{1,2,0:T(8,128)(2,1)S(1)}, bf16[2,128,768]{1,2,0:T(8,128)(2,1)S(1)}, u32[]{:S(2)}, u32[]{:S(2)}) %collective-permute-start) | collective-permute-done | bytes 393248 | tf_op jit(solution)/shard_map/while/body/eval_jaxpr/ppermute | solution.py:17
  117.0 0.7 copy-done.10
  117.9 0.8 slice_bitcast_fusion
  118.8 0.8 copy.58
  (135 shorter events, 4.7 us)
Async XLA Ops:
  1.4 0.7 copy-start.3
  3.1 0.9 copy-start
  24.7 1.2 copy-start.1
  43.1 1.2 copy-start.2
  60.8 0.5 copy-start.4
  61.4 0.6 copy-start.5
  62.0 0.8 copy-start.7
  62.0 0.8 copy-start.9
  67.4 9.6 %collective-permute-start = (bf16[2,128,768]{1,2,0:T(8,128)(2,1)S(1)}, bf16[2,128,768]{1,2,0:T(8,128)(2,1)S(1)}, u32[]{:S(2)}, u32[]{:S(2)}) collective-permute-start(bf16[2,128,768]{1,2,0:T(8,128)(2,1)S(1)} %fusion.64), channel_id=1, source_target_pairs={{24,0},{0,8},{8,16},{16,24},{25,1},{1,9},{9,17},{17,25},{26,2},{2,... | collective-permute-start | bytes 1179656 | tf_op jit(solution)/shard_map/while/body/eval_jaxpr/ppermute | solution.py:17
  77.1 0.7 copy-start.10
  77.1 0.7 copy-start.8
  77.1 0.7 copy-start.6
  77.8 0.8 copy-start.7
  77.8 0.8 copy-start.9
  78.9 11.0 %collective-permute-start = (bf16[2,128,768]{1,2,0:T(8,128)(2,1)S(1)}, bf16[2,128,768]{1,2,0:T(8,128)(2,1)S(1)}, u32[]{:S(2)}, u32[]{:S(2)}) collective-permute-start(bf16[2,128,768]{1,2,0:T(8,128)(2,1)S(1)} %fusion.64), channel_id=1, source_target_pairs={{24,0},{0,8},{8,16},{16,24},{25,1},{1,9},{9,17},{17,25},{26,2},{2,... | collective-permute-start | bytes 1179656 | tf_op jit(solution)/shard_map/while/body/eval_jaxpr/ppermute | solution.py:17
  89.9 0.7 copy-start.10
  89.9 0.7 copy-start.8
  90.0 0.7 copy-start.6
  90.6 0.8 copy-start.7
  90.6 0.8 copy-start.9
  91.7 11.1 %collective-permute-start = (bf16[2,128,768]{1,2,0:T(8,128)(2,1)S(1)}, bf16[2,128,768]{1,2,0:T(8,128)(2,1)S(1)}, u32[]{:S(2)}, u32[]{:S(2)}) collective-permute-start(bf16[2,128,768]{1,2,0:T(8,128)(2,1)S(1)} %fusion.64), channel_id=1, source_target_pairs={{24,0},{0,8},{8,16},{16,24},{25,1},{1,9},{9,17},{17,25},{26,2},{2,... | collective-permute-start | bytes 1179656 | tf_op jit(solution)/shard_map/while/body/eval_jaxpr/ppermute | solution.py:17
  102.9 0.7 copy-start.10
  102.9 0.7 copy-start.8
  102.9 0.7 copy-start.6
  103.6 0.8 copy-start.7
  103.6 0.8 copy-start.9
  104.7 12.2 %collective-permute-start = (bf16[2,128,768]{1,2,0:T(8,128)(2,1)S(1)}, bf16[2,128,768]{1,2,0:T(8,128)(2,1)S(1)}, u32[]{:S(2)}, u32[]{:S(2)}) collective-permute-start(bf16[2,128,768]{1,2,0:T(8,128)(2,1)S(1)} %fusion.64), channel_id=1, source_target_pairs={{24,0},{0,8},{8,16},{16,24},{25,1},{1,9},{9,17},{17,25},{26,2},{2,... | collective-permute-start | bytes 1179656 | tf_op jit(solution)/shard_map/while/body/eval_jaxpr/ppermute | solution.py:17
  117.0 0.7 copy-start.10
  117.0 0.7 copy-start.8
  117.0 0.7 copy-start.6
where the time goes:
time: 121 us; the launch traced here: 120 us
  blocking collectives  37.5 us (31%)
  waiting for transfers between devices  34.1 us (28%)
  matrix products  18.5 us (15%)
  local copies, waits for them, and re-layouts  11.3 us (9%)
  starting transfers between devices  9.41 us (8%)
  other arithmetic  4.46 us (4%)
  loops' own time  3.64 us (3%)
    ppermute x4, waiting for transfers between devices, passed_along(): return lax.ppermute(block, axis, route)  34.1 us
    all_gather x1, blocking collectives, body(): lax.all_gather(values, 'group', axis=0, tiled=True)  20.5 us
    all_gather x1, blocking collectives, body(): lax.all_gather(keys, 'group', axis=0, tiled=True)  17 us
    ppermute x4, starting transfers between devices, passed_along(): return lax.ppermute(block, axis, route)  9.41 us
    dot_general x6, matrix products, row_stats(): jnp.einsum('rd,kd->rk', query_head, key_head, preferred_element_type=jnp....  7.23 us
    dot_general x6, matrix products, row_stats(): jnp.dot(probs_low, value_head, preferred_element_type=jnp.float32)  7.23 us
    unnamed x18, local copies, waits for them, and re-layouts  6.1 us
    another operation x1, loops' own time, body(): lax.fori_loop(0, slice_count, chain_step, (query_zero, travel_zero))  3.34 us
  transfers between devices with their start and end apart: 4, of which 4 were waited for; matrix products, arithmetic and copies ran while one was open for 0% of the time, Pallas kernels for 0%

commit v1 on v0

--- a/solution.py
+++ b/solution.py
@@ -1,8 +1,11 @@
+import functools
 import math
 
 import jax
 import jax.numpy as jnp
 from jax import lax
+from jax.experimental import pallas as pl
+from jax.experimental.pallas import tpu as pltpu
 from jax.sharding import PartitionSpec as P
 
 HD = 128
@@ -133,10 +136,341 @@
     query_low = rows_first(query_grad * score_scale).astype(jnp.bfloat16)
     return (query_low, key_grad.astype(jnp.bfloat16), value_grad.astype(jnp.bfloat16))
 
+MESH = pl.DeviceIdType.MESH
+EXP_SCALE = 1.4426950408889634 / math.sqrt(HD)
+SCALE = 1.0 / math.sqrt(HD)
+
+
+def dot_nt(a, b):
+    return lax.dot_general(a, b, (((1,), (1,)), ((), ())), preferred_element_type=jnp.float32)
+
+
+def dot_nn(a, b):
+    return lax.dot_general(a, b, (((1,), (0,)), ((), ())), preferred_element_type=jnp.float32)
+
+
+def dot_tn(a, b):
+    return lax.dot_general(a, b, (((0,), (0,)), ((), ())), preferred_element_type=jnp.float32)
+
+
+def head_grads(query, grad, key, value, bias):
+    scores = dot_nt(key, query) * EXP_SCALE + bias
+    top = jnp.max(scores, axis=0, keepdims=True)
+    unnormed = jnp.exp2(scores - top)
+    total = jnp.sum(unnormed, axis=0, keepdims=True)
+    probs = unnormed * (1.0 / total)
+    prob_grad = dot_nt(value, grad)
+    delta = jnp.sum(probs * prob_grad, axis=0, keepdims=True)
+    score_grad = (probs * (prob_grad - delta)).astype(jnp.bfloat16)
+    value_grad = dot_nn(probs.astype(jnp.bfloat16), grad)
+    key_grad = dot_nn(score_grad, query) * SCALE
+    query_grad = dot_tn(score_grad, key) * SCALE
+    return query_grad, key_grad, value_grad
+
+
+def columns(head):
+    return pl.ds(pl.multiple_of(head * HD, HD), HD)
+
+
+def kernel(
+    head_count, lengths, q_hbm, k_hbm, v_hbm, g_hbm, dq_hbm, dk_hbm, dv_hbm,
+    q_own, k_own, v_own, g_own, landed, back, partial, own_sum, done, bias, kept,
+    load_sem, send_sem, land_sem, partial_send, partial_recv, final_send, final_recv, store_sem,
+):
+    me = lax.axis_index("group")
+    rows = q_hbm.shape[0]
+    spans = lengths.shape[0]
+    span_len = 4 * rows // spans
+    inputs = ((k_hbm, k_own), (v_hbm, v_own), (q_hbm, q_own), (g_hbm, g_own))
+    outputs = (dq_hbm, dk_hbm, dv_hbm)
+
+    def load(which):
+        return pltpu.make_async_copy(inputs[which][0], inputs[which][1], load_sem.at[which])
+
+    def store(which, head):
+        return pltpu.make_async_copy(
+            done.at[which, head], outputs[which].at[:, columns(head)], store_sem.at[which, head]
+        )
+
+    def forward(which, slot, sender_slot, target, head):
+        return pltpu.make_async_remote_copy(
+            src_ref=inputs[which][0].at[:, columns(head)],
+            dst_ref=landed.at[slot, head],
+            send_sem=send_sem.at[sender_slot, head],
+            recv_sem=land_sem.at[slot, head],
+            device_id={"group": target},
+            device_id_type=MESH,
+        )
+
+    def give_back(pair, lane, target, head):
+        return pltpu.make_async_remote_copy(
+            src_ref=back.at[pair, head],
+            dst_ref=partial.at[lane, head],
+            send_sem=partial_send.at[pair, head],
+            recv_sem=partial_recv.at[lane, head],
+            device_id={"group": target},
+            device_id_type=MESH,
+        )
+
+    def finish(which, head):
+        return pltpu.make_async_remote_copy(
+            src_ref=done.at[3 + which, head],
+            dst_ref=outputs[which].at[:, columns(head)],
+            send_sem=final_send.at[which, head],
+            recv_sem=final_recv.at[which, head],
+            device_id={"group": 3},
+            device_id_type=MESH,
+        )
+
+    def greet(peers):
+        barrier = pltpu.get_barrier_semaphore()
+        for peer in peers:
+            pl.semaphore_signal(barrier, inc=1, device_id={"group": peer}, device_id_type=MESH)
+        pl.semaphore_wait(barrier, len(peers))
+
+    def each_head(step):
+        lax.fori_loop(0, head_count, lambda head, carry: (step(head), carry)[1], 0)
+
+    def make_masks(first_query, query_count, key_count):
+        shape = (key_count, query_count)
+        key_at = lax.broadcasted_iota(jnp.int32, shape, 0)
+        query_at = lax.broadcasted_iota(jnp.int32, shape, 1) + first_query
+        row_at = lax.broadcasted_iota(jnp.int32, (query_count, HD), 0) + first_query
+        key_span = jnp.zeros(shape, jnp.int32)
+        query_span = jnp.zeros(shape, jnp.int32)
+        key_end = jnp.zeros(shape, jnp.int32)
+        row_end = jnp.zeros((query_count, HD), jnp.int32)
+        for span in range(spans):
+            start = span * span_len
+            end = start + lengths[span]
+            key_span = jnp.where(key_at >= start, span, key_span)
+            query_span = jnp.where(query_at >= start, span, query_span)
+            key_end = jnp.where(key_at >= start, end, key_end)
+            row_end = jnp.where(row_at >= start, end, row_end)
+        visible = (key_span <= query_span) & (key_at < key_end)
+        bias[:key_count, :query_count] = jnp.where(visible, 0.0, masked_score)
+        kept[:query_count, :] = jnp.where(row_at < row_end, 1.0, 0.0).astype(jnp.bfloat16)
+
+    for which in range(4):
+        load(which).start()
+
+    def wait_loads():
+        for which in range(4):
+            load(which).wait()
+
+    def low(value):
+        return value.astype(jnp.bfloat16)
+
+    @pl.when(me == 0)
+    def _():
+        greet((1, 2))
+
+        def send(head):
+            for which in range(2):
+                forward(which, which, which, 2, head).start()
+            for which in range(2):
+                forward(which, which, 2 + which, 1, head).start()
+
+        each_head(send)
+        make_masks(0, rows, rows)
+        wait_loads()
+
+        def own(head):
+            at = columns(head)
+            dq, dk, dv = head_grads(
+                q_own[:, at], g_own[:, at] * kept[:rows, :], k_own[:, at], v_own[:, at],
+                bias[:rows, :rows],
+            )
+            done[0, head] = low(dq)
+            own_sum[0, head] = dk
+            own_sum[1, head] = dv
+            store(0, head).start()
+
+        each_head(own)
+
+        def gather(head):
+            give_back(0, 0, 0, head).wait_recv()
+            give_back(0, 1, 0, head).wait_recv()
+            for which in range(2):
+                done[1 + which, head] = low(
+                    own_sum[which, head]
+                    + partial[0, head, which].astype(jnp.float32)
+                    + partial[1, head, which].astype(jnp.float32)
+                )
+                store(1 + which, head).start()
+
+        each_head(gather)
+
+        def settle(head):
+            for which in range(2):
+                forward(which, which, which, 2, head).wait_send()
+                forward(which, which, 2 + which, 1, head).wait_send()
+            for which in range(3):
+                store(which, head).wait()
+
+        each_head(settle)
+
+    @pl.when(me == 1)
+    def _():
+        greet((0, 2))
+
+        def send(head):
+            for which in range(2):
+                forward(which, 2 + which, which, 2, head).start()
+
+        each_head(send)
+        make_masks(rows, rows, 2 * rows)
+        wait_loads()
+
+        def work(head):
+            at = columns(head)
+            for which in range(2):
+                forward(which, which, 2 + which, 1, head).wait_recv()
+            dq, dk, dv = head_grads(
+                q_own[:, at], g_own[:, at] * kept[:rows, :],
+                jnp.concatenate([landed[0, head], k_own[:, at]], axis=0),
+                jnp.concatenate([landed[1, head], v_own[:, at]], axis=0),
+                bias[: 2 * rows, :rows],
+            )
+            back[0, head, 0] = low(dk[:rows])
+            back[0, head, 1] = low(dv[:rows])
+            give_back(0, 0, 0, head).start()
+            own_sum[0, head] = dk[rows:]
+            own_sum[1, head] = dv[rows:]
+            done[0, head] = low(dq)
+            store(0, head).start()
+
+        each_head(work)
+
+        def gather(head):
+            give_back(1, 0, 1, head).wait_recv()
+            for which in range(2):
+                done[1 + which, head] = low(
+                    own_sum[which, head] + partial[0, head, which].astype(jnp.float32)
+                )
+                store(1 + which, head).start()
+
+        each_head(gather)
+
+        def settle(head):
+            for which in range(2):
+                forward(which, 2 + which, which, 2, head).wait_send()
+            give_back(0, 0, 0, head).wait_send()
+            for which in range(3):
+                store(which, head).wait()
+
+        each_head(settle)
+
+    @pl.when(me == 2)
+    def _():
+        greet((0, 1, 3))
+        make_masks(2 * rows, 2 * rows, 4 * rows)
+        wait_loads()
+
+        def work(head):
+            at = columns(head)
+            for slot in range(4):
+                forward(slot % 2, slot, slot, 2, head).wait_recv()
+            for which in range(4):
+                forward(which, 4 + which, which, 2, head).wait_recv()
+            dq, dk, dv = head_grads(
+                jnp.concatenate([q_own[:, at], landed[6, head]], axis=0),
+                jnp.concatenate([g_own[:, at], landed[7, head]], axis=0) * kept[...],
+                jnp.concatenate(
+                    [landed[0, head], landed[2, head], k_own[:, at], landed[4, head]], axis=0
+                ),
+                jnp.concatenate(
+                    [landed[1, head], landed[3, head], v_own[:, at], landed[5, head]], axis=0
+                ),
+                bias[...],
+            )
+            for target in range(2):
+                mine = slice(target * rows, (target + 1) * rows)
+                back[target, head, 0] = low(dk[mine])
+                back[target, head, 1] = low(dv[mine])
+                give_back(target, 1 - target, target, head).start()
+            for which, grad in ((1, dk), (2, dv)):
+                done[which, head] = low(grad[2 * rows : 3 * rows])
+                done[3 + which, head] = low(grad[3 * rows :])
+            done[0, head] = low(dq[:rows])
+            done[3, head] = low(dq[rows:])
+            for which in range(3):
+                finish(which, head).start()
+                store(which, head).start()
+
+        each_head(work)
+
+        def settle(head):
+            for target in range(2):
+                give_back(target, 1 - target, target, head).wait_send()
+            for which in range(3):
+                finish(which, head).wait_send()
+                store(which, head).wait()
+
+        each_head(settle)
+
+    @pl.when(me == 3)
+    def _():
+        greet((2,))
+
+        def send(head):
+            for which in range(4):
+                forward(which, 4 + which, which, 2, head).start()
+
+        each_head(send)
+        wait_loads()
+
+        def settle(head):
+            for which in range(4):
+                forward(which, 4 + which, which, 2, head).wait_send()
+            for which in range(3):
+                finish(which, head).wait_recv()
+
+        each_head(settle)
+
+
+def four_slices(queries, keys, values, grad_out, lengths):
+    rows, features = queries.shape
+    heads = features // HD
+    low_type = jnp.bfloat16
+    out = jax.ShapeDtypeStruct((rows, features), low_type)
+    anywhere = pl.BlockSpec(memory_space=pl.ANY)
+    dma = pltpu.SemaphoreType.DMA
+    return pl.pallas_call(
+        functools.partial(kernel, heads),
+        out_shape=(out, out, out),
+        in_specs=[pl.BlockSpec(memory_space=pltpu.SMEM)] + [anywhere] * 4,
+        out_specs=(anywhere,) * 3,
+        scratch_shapes=[
+            pltpu.VMEM((rows, features), low_type),
+            pltpu.VMEM((rows, features), low_type),
+            pltpu.VMEM((rows, features), low_type),
+            pltpu.VMEM((rows, features), low_type),
+            pltpu.VMEM((8, heads, rows, HD), low_type),
+            pltpu.VMEM((2, heads, 2, rows, HD), low_type),
+            pltpu.VMEM((2, heads, 2, rows, HD), low_type),
+            pltpu.VMEM((2, heads, rows, HD), jnp.float32),
+            pltpu.VMEM((6, heads, rows, HD), low_type),
+            pltpu.VMEM((4 * rows, 2 * rows), jnp.float32),
+            pltpu.VMEM((2 * rows, HD), low_type),
+            dma((4,)),
+            dma((4, heads)),
+            dma((8, heads)),
+            dma((2, heads)),
+            dma((2, heads)),
+            dma((3, heads)),
+            dma((3, heads)),
+            dma((3, heads)),
+        ],
+        compiler_params=pltpu.CompilerParams(
+            collective_id=0, has_side_effects=True, vmem_limit_bytes=40 * 1024 * 1024
+        ),
+    )(lengths, queries, keys, values, grad_out)
+
 
 def solution(mesh):
     return jax.shard_map(
-        body,
+        four_slices if mesh.shape["group"] == 4 else body,
         mesh=mesh,
         in_specs=(
             P(("batch", "group"), "head"),

time: 121 us -> 37.9 us (0.31)
  blocking collectives: 37.5 us -> 0 us
  waiting for transfers between devices: 34.1 us -> 0 us
  Pallas kernels: 0 us -> 30.6 us
  matrix products: 18.5 us -> 0 us
  starting transfers between devices: 9.41 us -> 0 us
  local copies, waits for them, and re-layouts: 11.3 us -> 6.39 us
  other arithmetic: 4.46 us -> 0 us
  loops' own time: 3.64 us -> 0 us
    all_gather x2 -> x0, blocking collectives: 37.5 us -> none  [the longest x1 20.5 us: body(): lax.all_gather(values, 'group', axis=0, tiled=True)]
    ppermute x4 -> x0, waiting for transfers between devices: 34.1 us -> none  [passed_along(): return lax.ppermute(block, axis, route)]
    pallas_call x0 -> x1, Pallas kernels: none -> 30.6 us  [four_slices(): pl.pallas_call(functools.partial(kernel, heads), out_shape=(out, out, out...]
    dot_general x17 -> x0, matrix products: 18.5 us -> none  [the longest x6 7.23 us: row_stats(): jnp.einsum('rd,kd->rk', query_head, key_head, preferred_element_type=jnp....]
    ppermute x4 -> x0, starting transfers between devices: 9.41 us -> none  [passed_along(): return lax.ppermute(block, axis, route)]
    another operation x6 -> x0, loops' own time: 3.64 us -> none  [the longest x1 3.34 us: body(): lax.fori_loop(0, slice_count, chain_step, (query_zero, travel_zero))]
    while x42 -> x0, local copies, waits for them, and re-layouts: 3.09 us -> none
    select_n x5 -> x0, other arithmetic: 1.75 us -> none  [the longest x1 1.01 us: body(): jnp.where(own_valid[:, None], grad_out, jnp.zeros_like(grad_out))]
  transfers between devices with their start and end apart: 4 -> 0, of which waited for: 4 -> 0; matrix products, arithmetic and copies ran while one was open for 0% -> 0% of each run, Pallas kernels for 0% -> 0%
where the time goes in v1:
time: 37.9 us; the launch traced here: 37.6 us
  Pallas kernels  30.6 us (81%)
  local copies, waits for them, and re-layouts  6.39 us (17%)
  between operations  0.65 us (2%)
    pallas_call x1, Pallas kernels, four_slices(): pl.pallas_call(functools.partial(kernel, heads), out_shape=(out, out, out...  30.6 us
    unnamed x13, local copies, waits for them, and re-layouts  6.39 us

profile of v1, /device:TPU:0, one launch (start us, length us, event | category | flops | bytes accessed | tf_op | source)
XLA Modules:
  0.0 37.6 jit_solution(7312630724754054886)
XLA Ops:
  0.6 0.0 copy-start
  0.6 0.9 %copy-done = bf16[128,768]{1,0:T(8,128)(2,1)S(1)} copy-done((bf16[128,768]{1,0:T(8,128)(2,1)S(1)}, bf16[128,768]{1,0:T(8,128)(2,1)}, u32[]{:S(2)}) %copy-start) | copy-done | bytes 196632
  1.6 0.0 copy-start.1
  1.6 0.9 %copy-done.1 = bf16[128,768]{1,0:T(8,128)(2,1)S(1)} copy-done((bf16[128,768]{1,0:T(8,128)(2,1)S(1)}, bf16[128,768]{1,0:T(8,128)(2,1)}, u32[]{:S(2)}) %copy-start.1) | copy-done | bytes 196632
  2.5 0.0 copy-start.2
  2.5 0.9 %copy-done.2 = bf16[128,768]{1,0:T(8,128)(2,1)S(1)} copy-done((bf16[128,768]{1,0:T(8,128)(2,1)S(1)}, bf16[128,768]{1,0:T(8,128)(2,1)}, u32[]{:S(2)}) %copy-start.2) | copy-done | bytes 196632
  3.4 0.0 copy-start.3
  3.4 0.9 %copy-done.3 = bf16[128,768]{1,0:T(8,128)(2,1)S(1)} copy-done((bf16[128,768]{1,0:T(8,128)(2,1)S(1)}, bf16[128,768]{1,0:T(8,128)(2,1)}, u32[]{:S(2)}) %copy-start.3) | copy-done | bytes 196632
  4.3 0.0 copy-start.4
  4.3 0.7 %copy-done.4 = s32[8]{0:T(128)S(1)} copy-done((s32[8]{0:T(128)S(1)}, s32[8]{0:T(128)}, u32[]{:S(2)}) %copy-start.4) | copy-done | bytes 56
  5.0 30.6 %shard_map.76 = (bf16[128,768]{1,0:T(8,128)(2,1)S(1)}, bf16[128,768]{1,0:T(8,128)(2,1)S(1)}, bf16[128,768]{1,0:T(8,128)(2,1)S(1)}) custom-call(s32[8]{0:T(128)S(1)} %copy-done.4, bf16[128,768]{1,0:T(8,128)(2,1)S(1)} %copy-done, bf16[128,768]{1,0:T(8,128)(2,1)S(1)} %copy-done.1, bf16[128,768]{1,0:T(8,128)(2,1)S(1)} %copy-done.2, bf16[128,768]{1,0:T(8,128)(2,1)S(1)} %copy-done.3), custom_call_target="tpu_custom_call" | custom-call | tf_op jit(solution)/shard_map/pallas_call | solution.py:439
  35.6 0.7 %copy.11 = bf16[128,768]{1,0:T(8,128)(2,1)} copy(bf16[128,768]{1,0:T(8,128)(2,1)S(1)} %get-tuple-element.6) | data formatting | bytes 393216
  36.3 0.7 %copy.12 = bf16[128,768]{1,0:T(8,128)(2,1)} copy(bf16[128,768]{1,0:T(8,128)(2,1)S(1)} %get-tuple-element.7) | data formatting | bytes 393216
  37.0 0.7 %copy.13 = bf16[128,768]{1,0:T(8,128)(2,1)} copy(bf16[128,768]{1,0:T(8,128)(2,1)S(1)} %get-tuple-element.8) | data formatting | bytes 393216
Async XLA Ops:
  0.6 0.9 %copy-start = (bf16[128,768]{1,0:T(8,128)(2,1)S(1)}, bf16[128,768]{1,0:T(8,128)(2,1)}, u32[]{:S(2)}) copy-start(bf16[128,768]{1,0:T(8,128)(2,1)} %q_hbm.1) | copy-start | bytes 589828
  1.6 0.9 %copy-start.1 = (bf16[128,768]{1,0:T(8,128)(2,1)S(1)}, bf16[128,768]{1,0:T(8,128)(2,1)}, u32[]{:S(2)}) copy-start(bf16[128,768]{1,0:T(8,128)(2,1)} %k_hbm.1) | copy-start | bytes 589828
  2.5 0.9 %copy-start.2 = (bf16[128,768]{1,0:T(8,128)(2,1)S(1)}, bf16[128,768]{1,0:T(8,128)(2,1)}, u32[]{:S(2)}) copy-start(bf16[128,768]{1,0:T(8,128)(2,1)} %v_hbm.1) | copy-start | bytes 589828
  3.4 0.9 %copy-start.3 = (bf16[128,768]{1,0:T(8,128)(2,1)S(1)}, bf16[128,768]{1,0:T(8,128)(2,1)}, u32[]{:S(2)}) copy-start(bf16[128,768]{1,0:T(8,128)(2,1)} %g_hbm.1) | copy-start | bytes 589828
  4.3 0.7 %copy-start.4 = (s32[8]{0:T(128)S(1)}, s32[8]{0:T(128)}, u32[]{:S(2)}) copy-start(s32[8]{0:T(128)} %lengths.1) | copy-start | bytes 100

commit v2 on v1

--- a/solution.py
+++ b/solution.py
@@ -429,6 +429,12 @@
         each_head(settle)
 
 
+def hand_over(dq, dk, dv, dq_out, dk_out, dv_out):
+    dq_out[...] = dq[...]
+    dk_out[...] = dk[...]
+    dv_out[...] = dv[...]
+
+
 def four_slices(queries, keys, values, grad_out, lengths):
     rows, features = queries.shape
     heads = features // HD
@@ -436,7 +442,7 @@
     out = jax.ShapeDtypeStruct((rows, features), low_type)
     anywhere = pl.BlockSpec(memory_space=pl.ANY)
     dma = pltpu.SemaphoreType.DMA
-    return pl.pallas_call(
+    grads = pl.pallas_call(
         functools.partial(kernel, heads),
         out_shape=(out, out, out),
         in_specs=[pl.BlockSpec(memory_space=pltpu.SMEM)] + [anywhere] * 4,
@@ -463,9 +469,15 @@
             dma((3, heads)),
         ],
         compiler_params=pltpu.CompilerParams(
-            collective_id=0, has_side_effects=True, vmem_limit_bytes=40 * 1024 * 1024
+            collective_id=0, has_side_effects=True, vmem_limit_bytes=60 * 1024 * 1024
         ),
     )(lengths, queries, keys, values, grad_out)
+    return pl.pallas_call(
+        hand_over,
+        out_shape=(out, out, out),
+        in_specs=[pl.BlockSpec(memory_space=pltpu.VMEM)] * 3,
+        out_specs=(pl.BlockSpec(memory_space=pltpu.VMEM),) * 3,
+    )(*grads)
 
 
 def solution(mesh):

time: 37.9 us -> 33.2 us (0.88)
  local copies, waits for them, and re-layouts: 6.39 us -> 0 us
  Pallas kernels: 30.6 us -> 32.4 us
    unnamed x13 -> x0, local copies, waits for them, and re-layouts: 6.39 us -> none
    pallas_call x0 -> x1, Pallas kernels: none -> 1.94 us  [four_slices(): pl.pallas_call(hand_over, out_shape=(out, out, out), in_specs=[pl.BlockSp...]
where the time goes in v2:
time: 33.2 us; the launch traced here: 33 us
  Pallas kernels  32.4 us (98%)
  between operations  0.64 us (2%)
    pallas_call x1, Pallas kernels, four_slices(): pl.pallas_call(functools.partial(kernel, heads), out_shape=(out, out, out...  30.5 us
    pallas_call x1, Pallas kernels, four_slices(): pl.pallas_call(hand_over, out_shape=(out, out, out), in_specs=[pl.BlockSp...  1.94 us

profile of v2, /device:TPU:0, one launch (start us, length us, event | category | flops | bytes accessed | tf_op | source)
XLA Modules:
  0.0 33.0 jit_solution(6561096761844151012)
XLA Ops:
  0.6 30.5 %shard_map.76 = (bf16[128,768]{1,0:T(8,128)(2,1)}, bf16[128,768]{1,0:T(8,128)(2,1)}, bf16[128,768]{1,0:T(8,128)(2,1)}) custom-call(s32[8]{0:T(128)} %lengths.1, bf16[128,768]{1,0:T(8,128)(2,1)} %q_hbm.1, bf16[128,768]{1,0:T(8,128)(2,1)} %k_hbm.1, bf16[128,768]{1,0:T(8,128)(2,1)} %v_hbm.1, bf16[128,768]{1,0:T(8,128)(2,1)} %g_hbm.1), custom_call_target="tpu_custom_call" | custom-call | tf_op jit(solution)/shard_map/pallas_call | solution.py:445
  31.1 1.9 %shard_map.77 = (bf16[128,768]{1,0:T(8,128)(2,1)}, bf16[128,768]{1,0:T(8,128)(2,1)}, bf16[128,768]{1,0:T(8,128)(2,1)}) custom-call(bf16[128,768]{1,0:T(8,128)(2,1)} %get-tuple-element.6.dq, bf16[128,768]{1,0:T(8,128)(2,1)} %get-tuple-element.7.dk, bf16[128,768]{1,0:T(8,128)(2,1)} %get-tuple-element.8.dv), custom_call_target="tpu_custom_call" | custom-call | tf_op jit(solution)/shard_map/pallas_call | solution.py:475

commit v3 on v1

--- a/solution.py
+++ b/solution.py
@@ -153,19 +153,18 @@
     return lax.dot_general(a, b, (((0,), (0,)), ((), ())), preferred_element_type=jnp.float32)
 
 
-def head_grads(query, grad, key, value, bias):
+def head_probs(query, key, bias):
     scores = dot_nt(key, query) * EXP_SCALE + bias
     top = jnp.max(scores, axis=0, keepdims=True)
     unnormed = jnp.exp2(scores - top)
     total = jnp.sum(unnormed, axis=0, keepdims=True)
-    probs = unnormed * (1.0 / total)
+    return unnormed * (1.0 / total)
+
+
+def head_score_grad(probs, grad, value):
     prob_grad = dot_nt(value, grad)
     delta = jnp.sum(probs * prob_grad, axis=0, keepdims=True)
-    score_grad = (probs * (prob_grad - delta)).astype(jnp.bfloat16)
-    value_grad = dot_nn(probs.astype(jnp.bfloat16), grad)
-    key_grad = dot_nn(score_grad, query) * SCALE
-    query_grad = dot_tn(score_grad, key) * SCALE
-    return query_grad, key_grad, value_grad
+    return (probs * (prob_grad - delta)).astype(jnp.bfloat16)
 
 
 def columns(head):
@@ -173,24 +172,19 @@
 
 
 def kernel(
-    head_count, lengths, q_hbm, k_hbm, v_hbm, g_hbm, dq_hbm, dk_hbm, dv_hbm,
+    head_count, lengths, q_hbm, k_hbm, v_hbm, g_hbm, dq_out_ref, dk_out_ref, dv_out_ref,
     q_own, k_own, v_own, g_own, landed, back, partial, own_sum, done, bias, kept,
-    load_sem, send_sem, land_sem, partial_send, partial_recv, final_send, final_recv, store_sem,
+    load_sem, send_sem, land_sem, partial_send, partial_recv, final_send, final_recv,
 ):
     me = lax.axis_index("group")
     rows = q_hbm.shape[0]
     spans = lengths.shape[0]
     span_len = 4 * rows // spans
     inputs = ((k_hbm, k_own), (v_hbm, v_own), (q_hbm, q_own), (g_hbm, g_own))
-    outputs = (dq_hbm, dk_hbm, dv_hbm)
+    outputs = (dq_out_ref, dk_out_ref, dv_out_ref)
 
     def load(which):
         return pltpu.make_async_copy(inputs[which][0], inputs[which][1], load_sem.at[which])
-
-    def store(which, head):
-        return pltpu.make_async_copy(
-            done.at[which, head], outputs[which].at[:, columns(head)], store_sem.at[which, head]
-        )
 
     def forward(which, slot, sender_slot, target, head):
         return pltpu.make_async_remote_copy(
@@ -202,19 +196,19 @@
             device_id_type=MESH,
         )
 
-    def give_back(pair, lane, target, head):
+    def give_back(pair, lane, which, target, head):
         return pltpu.make_async_remote_copy(
-            src_ref=back.at[pair, head],
-            dst_ref=partial.at[lane, head],
-            send_sem=partial_send.at[pair, head],
-            recv_sem=partial_recv.at[lane, head],
+            src_ref=back.at[pair, which, head],
+            dst_ref=partial.at[lane, which, head],
+            send_sem=partial_send.at[pair, which, head],
+            recv_sem=partial_recv.at[lane, which, head],
             device_id={"group": target},
             device_id_type=MESH,
         )
 
     def finish(which, head):
         return pltpu.make_async_remote_copy(
-            src_ref=done.at[3 + which, head],
+            src_ref=done.at[which, head],
             dst_ref=outputs[which].at[:, columns(head)],
             send_sem=final_send.at[which, head],
             recv_sem=final_recv.at[which, head],
@@ -277,27 +271,26 @@
 
         def own(head):
             at = columns(head)
-            dq, dk, dv = head_grads(
-                q_own[:, at], g_own[:, at] * kept[:rows, :], k_own[:, at], v_own[:, at],
-                bias[:rows, :rows],
-            )
-            done[0, head] = low(dq)
-            own_sum[0, head] = dk
-            own_sum[1, head] = dv
-            store(0, head).start()
+            query, key = q_own[:, at], k_own[:, at]
+            grad = g_own[:, at] * kept[:rows, :]
+            probs = head_probs(query, key, bias[:rows, :rows])
+            own_sum[1, head] = dot_nn(low(probs), grad)
+            score_grad = head_score_grad(probs, grad, v_own[:, at])
+            own_sum[0, head] = dot_nn(score_grad, query) * SCALE
+            dq_out_ref[:, at] = low(dot_tn(score_grad, key) * SCALE)
 
         each_head(own)
 
         def gather(head):
-            give_back(0, 0, 0, head).wait_recv()
-            give_back(0, 1, 0, head).wait_recv()
-            for which in range(2):
-                done[1 + which, head] = low(
+            at = columns(head)
+            for which in (1, 0):
+                give_back(0, 0, which, 0, head).wait_recv()
+                give_back(0, 1, which, 0, head).wait_recv()
+                outputs[1 + which][:, at] = low(
                     own_sum[which, head]
-                    + partial[0, head, which].astype(jnp.float32)
-                    + partial[1, head, which].astype(jnp.float32)
+                    + partial[0, which, head].astype(jnp.float32)
+                    + partial[1, which, head].astype(jnp.float32)
                 )
-                store(1 + which, head).start()
 
         each_head(gather)
 
@@ -305,8 +298,6 @@
             for which in range(2):
                 forward(which, which, which, 2, head).wait_send()
                 forward(which, which, 2 + which, 1, head).wait_send()
-            for which in range(3):
-                store(which, head).wait()
 
         each_head(settle)
 
@@ -324,40 +315,41 @@
 
         def work(head):
             at = columns(head)
-            for which in range(2):
-                forward(which, which, 2 + which, 1, head).wait_recv()
-            dq, dk, dv = head_grads(
-                q_own[:, at], g_own[:, at] * kept[:rows, :],
-                jnp.concatenate([landed[0, head], k_own[:, at]], axis=0),
-                jnp.concatenate([landed[1, head], v_own[:, at]], axis=0),
-                bias[: 2 * rows, :rows],
-            )
-            back[0, head, 0] = low(dk[:rows])
-            back[0, head, 1] = low(dv[:rows])
-            give_back(0, 0, 0, head).start()
+            query = q_own[:, at]
+            grad = g_own[:, at] * kept[:rows, :]
+            forward(0, 0, 2, 1, head).wait_recv()
+            key = jnp.concatenate([landed[0, head], k_own[:, at]], axis=0)
+            probs = head_probs(query, key, bias[: 2 * rows, :rows])
+            dv = dot_nn(low(probs), grad)
+            back[0, 1, head] = low(dv[:rows])
+            give_back(0, 0, 1, 0, head).start()
+            own_sum[1, head] = dv[rows:]
+            forward(1, 1, 3, 1, head).wait_recv()
+            value = jnp.concatenate([landed[1, head], v_own[:, at]], axis=0)
+            score_grad = head_score_grad(probs, grad, value)
+            dk = dot_nn(score_grad, query) * SCALE
+            back[0, 0, head] = low(dk[:rows])
+            give_back(0, 0, 0, 0, head).start()
             own_sum[0, head] = dk[rows:]
-            own_sum[1, head] = dv[rows:]
-            done[0, head] = low(dq)
-            store(0, head).start()
+            dq_out_ref[:, at] = low(dot_tn(score_grad, key) * SCALE)
 
         each_head(work)
 
         def gather(head):
-            give_back(1, 0, 1, head).wait_recv()
-            for which in range(2):
-                done[1 + which, head] = low(
-                    own_sum[which, head] + partial[0, head, which].astype(jnp.float32)
+            at = columns(head)
+            for which in (1, 0):
+                give_back(1, 0, which, 1, head).wait_recv()
+                outputs[1 + which][:, at] = low(
+                    own_sum[which, head] + partial[0, which, head].astype(jnp.float32)
                 )
-                store(1 + which, head).start()
 
         each_head(gather)
 
         def settle(head):
             for which in range(2):
                 forward(which, 2 + which, which, 2, head).wait_send()
-            give_back(0, 0, 0, head).wait_send()
-            for which in range(3):
-                store(which, head).wait()
+            for which in range(2):
+                give_back(0, 0, which, 0, head).wait_send()
 
         each_head(settle)
 
@@ -369,43 +361,52 @@
 
         def work(head):
             at = columns(head)
-            for slot in range(4):
-                forward(slot % 2, slot, slot, 2, head).wait_recv()
-            for which in range(4):
-                forward(which, 4 + which, which, 2, head).wait_recv()
-            dq, dk, dv = head_grads(
-                jnp.concatenate([q_own[:, at], landed[6, head]], axis=0),
-                jnp.concatenate([g_own[:, at], landed[7, head]], axis=0) * kept[...],
-                jnp.concatenate(
-                    [landed[0, head], landed[2, head], k_own[:, at], landed[4, head]], axis=0
-                ),
-                jnp.concatenate(
-                    [landed[1, head], landed[3, head], v_own[:, at], landed[5, head]], axis=0
-                ),
-                bias[...],
+
+            def arrive(which, slot):
+                forward(which, slot, which, 2, head).wait_recv()
+
+            def give(which, grad_sum):
+                for target in range(2):
+                    mine = slice(target * rows, (target + 1) * rows)
+                    back[target, which, head] = low(grad_sum[mine])
+                    give_back(target, 1 - target, which, target, head).start()
+                done[1 + which, head] = low(grad_sum[3 * rows :])
+                finish(1 + which, head).start()
+                outputs[1 + which][:, at] = low(grad_sum[2 * rows : 3 * rows])
+
+            arrive(2, 6)
+            arrive(3, 7)
+            arrive(0, 4)
+            arrive(0, 0)
+            arrive(0, 2)
+            query = jnp.concatenate([q_own[:, at], landed[6, head]], axis=0)
+            grad = jnp.concatenate([g_own[:, at], landed[7, head]], axis=0) * kept[...]
+            key = jnp.concatenate(
+                [landed[0, head], landed[2, head], k_own[:, at], landed[4, head]], axis=0
             )
-            for target in range(2):
-                mine = slice(target * rows, (target + 1) * rows)
-                back[target, head, 0] = low(dk[mine])
-                back[target, head, 1] = low(dv[mine])
-                give_back(target, 1 - target, target, head).start()
-            for which, grad in ((1, dk), (2, dv)):
-                done[which, head] = low(grad[2 * rows : 3 * rows])
-                done[3 + which, head] = low(grad[3 * rows :])
-            done[0, head] = low(dq[:rows])
-            done[3, head] = low(dq[rows:])
-            for which in range(3):
-                finish(which, head).start()
-                store(which, head).start()
+            probs = head_probs(query, key, bias[...])
+            give(1, dot_nn(low(probs), grad))
+            arrive(1, 5)
+            arrive(1, 1)
+            arrive(1, 3)
+            value = jnp.concatenate(
+                [landed[1, head], landed[3, head], v_own[:, at], landed[5, head]], axis=0
+            )
+            score_grad = head_score_grad(probs, grad, value)
+            give(0, dot_nn(score_grad, query) * SCALE)
+            dq = dot_tn(score_grad, key) * SCALE
+            dq_out_ref[:, at] = low(dq[:rows])
+            done[0, head] = low(dq[rows:])
+            finish(0, head).start()
 
         each_head(work)
 
         def settle(head):
             for target in range(2):
-                give_back(target, 1 - target, target, head).wait_send()
+                for which in range(2):
+                    give_back(target, 1 - target, which, target, head).wait_send()
             for which in range(3):
                 finish(which, head).wait_send()
-                store(which, head).wait()
 
         each_head(settle)
 
@@ -414,7 +415,7 @@
         greet((2,))
 
         def send(head):
-            for which in range(4):
+            for which in (0, 2, 3, 1):
                 forward(which, 4 + which, which, 2, head).start()
 
         each_head(send)
@@ -438,32 +439,31 @@
     dma = pltpu.SemaphoreType.DMA
     return pl.pallas_call(
         functools.partial(kernel, heads),
-        out_shape=(out, out, out),
+        out_shape=(pltpu.VMEM((rows, features), low_type),) * 3,
         in_specs=[pl.BlockSpec(memory_space=pltpu.SMEM)] + [anywhere] * 4,
-        out_specs=(anywhere,) * 3,
+        out_specs=(pl.BlockSpec(memory_space=pltpu.VMEM),) * 3,
         scratch_shapes=[
             pltpu.VMEM((rows, features), low_type),
             pltpu.VMEM((rows, features), low_type),
             pltpu.VMEM((rows, features), low_type),
             pltpu.VMEM((rows, features), low_type),
             pltpu.VMEM((8, heads, rows, HD), low_type),
-            pltpu.VMEM((2, heads, 2, rows, HD), low_type),
-            pltpu.VMEM((2, heads, 2, rows, HD), low_type),
+            pltpu.VMEM((2, 2, heads, rows, HD), low_type),
+            pltpu.VMEM((2, 2, heads, rows, HD), low_type),
             pltpu.VMEM((2, heads, rows, HD), jnp.float32),
-            pltpu.VMEM((6, heads, rows, HD), low_type),
+            pltpu.VMEM((3, heads, rows, HD), low_type),
             pltpu.VMEM((4 * rows, 2 * rows), jnp.float32),
             pltpu.VMEM((2 * rows, HD), low_type),
             dma((4,)),
             dma((4, heads)),
             dma((8, heads)),
-            dma((2, heads)),
-            dma((2, heads)),
-            dma((3, heads)),
+            dma((2, 2, heads)),
+            dma((2, 2, heads)),
             dma((3, heads)),
             dma((3, heads)),
         ],
         compiler_params=pltpu.CompilerParams(
-            collective_id=0, has_side_effects=True, vmem_limit_bytes=40 * 1024 * 1024
+            collective_id=0, has_side_effects=True, vmem_limit_bytes=60 * 1024 * 1024
         ),
     )(lengths, queries, keys, values, grad_out)
 

time: 37.9 us -> 32.3 us (0.85)
  local copies, waits for them, and re-layouts: 6.39 us -> 2.03 us
  Pallas kernels: 30.6 us -> 29.5 us
    unnamed x13 -> x3, local copies, waits for them, and re-layouts: 6.39 us -> 2.03 us
    pallas_call x1, Pallas kernels: 30.6 us -> 29.5 us  [four_slices(): pl.pallas_call(functools.partial(kernel, heads), out_shape=(pltpu.VMEM((r...]
where the time goes in v3:
time: 32.3 us; the launch traced here: 32.1 us
  Pallas kernels  29.5 us (91%)
  local copies, waits for them, and re-layouts  2.03 us (6%)
  between operations  0.64 us (2%)
    pallas_call x1, Pallas kernels, four_slices(): pl.pallas_call(functools.partial(kernel, heads), out_shape=(pltpu.VMEM((r...  29.5 us
    unnamed x3, local copies, waits for them, and re-layouts  2.03 us

profile of v3, /device:TPU:0, one launch (start us, length us, event | category | flops | bytes accessed | tf_op | source)
XLA Modules:
  0.0 32.1 jit_solution(9588041318130859147)
XLA Ops:
  0.6 29.5 %shard_map.76 = (bf16[128,768]{1,0:T(8,128)(2,1)S(1)}, bf16[128,768]{1,0:T(8,128)(2,1)S(1)}, bf16[128,768]{1,0:T(8,128)(2,1)S(1)}) custom-call(s32[8]{0:T(128)} %lengths.1, bf16[128,768]{1,0:T(8,128)(2,1)} %q_hbm.1, bf16[128,768]{1,0:T(8,128)(2,1)} %k_hbm.1, bf16[128,768]{1,0:T(8,128)(2,1)} %v_hbm.1, bf16[128,768]{1,0:T(8,128)(2,1)} %g_hbm.1), custom_call_target="tpu_custom_call" | custom-call | tf_op jit(solution)/shard_map/pallas_call | solution.py:440
  30.1 0.7 %copy.11 = bf16[128,768]{1,0:T(8,128)(2,1)} copy(bf16[128,768]{1,0:T(8,128)(2,1)S(1)} %get-tuple-element.3) | data formatting | bytes 393216
  30.8 0.7 %copy.12 = bf16[128,768]{1,0:T(8,128)(2,1)} copy(bf16[128,768]{1,0:T(8,128)(2,1)S(1)} %get-tuple-element.4) | data formatting | bytes 393216
  31.5 0.7 %copy.13 = bf16[128,768]{1,0:T(8,128)(2,1)} copy(bf16[128,768]{1,0:T(8,128)(2,1)S(1)} %get-tuple-element.5) | data formatting | bytes 393216

commit v4 on v3

--- a/solution.py
+++ b/solution.py
@@ -261,9 +261,8 @@
 
         def send(head):
             for which in range(2):
+                forward(which, which, 2 + which, 1, head).start()
                 forward(which, which, which, 2, head).start()
-            for which in range(2):
-                forward(which, which, 2 + which, 1, head).start()
 
         each_head(send)
         make_masks(0, rows, rows)

time: 32.3 us -> 32.1 us (level)
  no operation moved by 1% of the time
where the time goes in v4:
time: 32.1 us; the launch traced here: 32 us
  Pallas kernels  29.3 us (91%)
  local copies, waits for them, and re-layouts  2.03 us (6%)
  between operations  0.64 us (2%)
    pallas_call x1, Pallas kernels, four_slices(): pl.pallas_call(functools.partial(kernel, heads), out_shape=(pltpu.VMEM((r...  29.3 us
    unnamed x3, local copies, waits for them, and re-layouts  2.03 us

profile of v4, /device:TPU:0, one launch (start us, length us, event | category | flops | bytes accessed | tf_op | source)
XLA Modules:
  0.0 32.0 jit_solution(9288393352543555549)
XLA Ops:
  0.6 29.3 %shard_map.76 = (bf16[128,768]{1,0:T(8,128)(2,1)S(1)}, bf16[128,768]{1,0:T(8,128)(2,1)S(1)}, bf16[128,768]{1,0:T(8,128)(2,1)S(1)}) custom-call(s32[8]{0:T(128)} %lengths.1, bf16[128,768]{1,0:T(8,128)(2,1)} %q_hbm.1, bf16[128,768]{1,0:T(8,128)(2,1)} %k_hbm.1, bf16[128,768]{1,0:T(8,128)(2,1)} %v_hbm.1, bf16[128,768]{1,0:T(8,128)(2,1)} %g_hbm.1), custom_call_target="tpu_custom_call" | custom-call | tf_op jit(solution)/shard_map/pallas_call | solution.py:439
  30.0 0.7 %copy.11 = bf16[128,768]{1,0:T(8,128)(2,1)} copy(bf16[128,768]{1,0:T(8,128)(2,1)S(1)} %get-tuple-element.3) | data formatting | bytes 393216
  30.6 0.7 %copy.12 = bf16[128,768]{1,0:T(8,128)(2,1)} copy(bf16[128,768]{1,0:T(8,128)(2,1)S(1)} %get-tuple-element.4) | data formatting | bytes 393216
  31.3 0.7 %copy.13 = bf16[128,768]{1,0:T(8,128)(2,1)} copy(bf16[128,768]{1,0:T(8,128)(2,1)S(1)} %get-tuple-element.5) | data formatting | bytes 393216

commit v5 on v4

--- a/solution.py
+++ b/solution.py
@@ -245,8 +245,10 @@
         bias[:key_count, :query_count] = jnp.where(visible, 0.0, masked_score)
         kept[:query_count, :] = jnp.where(row_at < row_end, 1.0, 0.0).astype(jnp.bfloat16)
 
-    for which in range(4):
-        load(which).start()
+    @pl.when(me != 3)
+    def _():
+        for which in range(4):
+            load(which).start()
 
     def wait_loads():
         for which in range(4):
@@ -418,7 +420,6 @@
                 forward(which, 4 + which, which, 2, head).start()
 
         each_head(send)
-        wait_loads()
 
         def settle(head):
             for which in range(4):

time: 32.1 us -> 32.1 us (level)
  no operation moved by 1% of the time
where the time goes in v5:
time: 32.1 us; the launch traced here: 32 us
  Pallas kernels  29.3 us (91%)
  local copies, waits for them, and re-layouts  2.03 us (6%)
  between operations  0.64 us (2%)
    pallas_call x1, Pallas kernels, four_slices(): pl.pallas_call(functools.partial(kernel, heads), out_shape=(pltpu.VMEM((r...  29.3 us
    unnamed x3, local copies, waits for them, and re-layouts  2.03 us

profile of v5, /device:TPU:0, one launch (start us, length us, event | category | flops | bytes accessed | tf_op | source)
XLA Modules:
  0.0 32.0 jit_solution(2300718287541891962)
XLA Ops:
  0.6 29.3 %shard_map.76 = (bf16[128,768]{1,0:T(8,128)(2,1)S(1)}, bf16[128,768]{1,0:T(8,128)(2,1)S(1)}, bf16[128,768]{1,0:T(8,128)(2,1)S(1)}) custom-call(s32[8]{0:T(128)} %lengths.1, bf16[128,768]{1,0:T(8,128)(2,1)} %q_hbm.1, bf16[128,768]{1,0:T(8,128)(2,1)} %k_hbm.1, bf16[128,768]{1,0:T(8,128)(2,1)} %v_hbm.1, bf16[128,768]{1,0:T(8,128)(2,1)} %g_hbm.1), custom_call_target="tpu_custom_call" | custom-call | tf_op jit(solution)/shard_map/pallas_call | solution.py:440
  30.0 0.7 %copy.11 = bf16[128,768]{1,0:T(8,128)(2,1)} copy(bf16[128,768]{1,0:T(8,128)(2,1)S(1)} %get-tuple-element.3) | data formatting | bytes 393216
  30.6 0.7 %copy.12 = bf16[128,768]{1,0:T(8,128)(2,1)} copy(bf16[128,768]{1,0:T(8,128)(2,1)S(1)} %get-tuple-element.4) | data formatting | bytes 393216
  31.3 0.7 %copy.13 = bf16[128,768]{1,0:T(8,128)(2,1)} copy(bf16[128,768]{1,0:T(8,128)(2,1)S(1)} %get-tuple-element.5) | data formatting | bytes 393216
